TPU v7x, 256 devices: a whole 4x4x8 slice. The times are simulated.
256 devices in a mesh: grp: 8 (over x, core), shard: 32 (over y, z).
Axes of the slice: x: 4, y: 4, z: 8, core: 2. Of those that a mesh axis runs over, the one named last changes fastest.
Arguments:
- inputs: bfloat16 [2, 1024, 4096], P(None, None, 'grp'), may hold values from -6 to 6
- up_cotangent: bfloat16 [2, 1024, 14336], P(None, None, 'shard'), may hold values from -0.1875 to 0.1875
- signs: int32 [4096, 16384], P('grp', 'shard'), may hold values from -1 to 1, as said below
- kept_row: int32 [8192], replicated, may hold values from 0 to 4095
- kept_col: int32 [8192], replicated, may hold values from 0 to 16383
Outputs:
- features: float32 [2, 8192], P(None, ('grp', 'shard'))
Inputs may be any that keep to these rules, and one draw needn't show every extreme that they name: `signs`: every entry is -1 or +1.
All inputs are finite; a program needn't handle non-finite values.
Results may differ from a plain program's by a relative error of at most 0.0003.
Values sent between devices are 32-bit elements; how exact they have to be, the bound alone decides.
A program may use at most 320 MiB of HBM per device.

v0:
```python
import math

import jax
import jax.numpy as jnp
from jax import lax
from jax.sharding import PartitionSpec as P

D = 4096
FPAD = 16384


def partner_2(block, axis, apart):
    count = lax.axis_size(axis)
    route = []
    for low in range(count):
        high = low | 1 << apart
        if high != low and high < count:
            route += [(low, high), (high, low)]
    return lax.ppermute(block, axis, route)


def hadamard_table(length):
    indices = jnp.arange(length, dtype=jnp.int32)
    parity = jnp.zeros((length, length), jnp.int32)
    for bit_number in range(length.bit_length() - 1):
        left_bits = jnp.bitwise_and(jnp.right_shift(indices, bit_number), 1)
        parity = parity + left_bits[:, None] * left_bits[None, :]
    return (1 - 2 * (parity % 2)).astype(jnp.float32)


def local(inputs, up_cotangent, signs, kept_row, kept_col):
    examples = inputs.shape[0]
    row_count = inputs.shape[2]
    unit_count = up_cotangent.shape[2]
    column_count = signs.shape[1]
    scale = 1.0 / math.sqrt(D * FPAD)
    gradient = jnp.einsum("etd,etf->edf", inputs, up_cotangent, preferred_element_type=jnp.float32)
    placed = jnp.pad(gradient, ((0, 0), (0, 0), (0, column_count - unit_count)))
    values = placed * signs.astype(jnp.float32)[None]
    row_table = hadamard_table(row_count)
    column_table = hadamard_table(column_count)
    values = jnp.einsum("ir,erc->eic", row_table, values, precision=lax.Precision.HIGHEST)
    values = jnp.einsum("erc,cj->erj", values, column_table, precision=lax.Precision.HIGHEST)
    position = lax.axis_index("shard")
    for bit_number in range(lax.axis_size("shard").bit_length() - 1):
        partner = partner_2(values, "shard", bit_number)
        upper_half = jnp.bitwise_and(jnp.right_shift(position, bit_number), 1) == 1
        values = jnp.where(upper_half, partner - values, values + partner)
    position = lax.axis_index("grp")
    for bit_number in range(lax.axis_size("grp").bit_length() - 1):
        partner = partner_2(values, "grp", bit_number)
        upper_half = jnp.bitwise_and(jnp.right_shift(position, bit_number), 1) == 1
        values = jnp.where(upper_half, partner - values, values + partner)
    local_row = kept_row - lax.axis_index("grp") * row_count
    local_col = kept_col - lax.axis_index("shard") * column_count
    inside = (
        (local_row >= 0) & (local_row < row_count) & (local_col >= 0) & (local_col < column_count)
    )
    flat_index = jnp.clip(local_row, 0, row_count - 1) * column_count + jnp.clip(
        local_col, 0, column_count - 1
    )
    picked = jnp.take(values.reshape(examples, row_count * column_count), flat_index, axis=1)
    share_term = jnp.where(inside[None, :], picked, 0.0) * scale
    return lax.psum_scatter(share_term, ("grp", "shard"), scatter_dimension=1, tiled=True)


def solution(mesh):
    placed = (P(None, None, "grp"), P(None, None, "shard"), P("grp", "shard"), P(), P())
    return jax.shard_map(
        local, mesh=mesh, in_specs=placed, out_specs=P(None, ("grp", "shard")), check_vma=False
    )
```

profile of v0, /device:TPU:0, one launch (start us, length us, event | category | flops | bytes accessed | tf_op | source)
XLA Modules:
  0.0 2172.0 jit_solution(17981930503116095829)
XLA Ops:
  10.6 4.7 fusion.2
  15.3 6.0 fusion
  21.5 45.9 %collective-permute-done = f32[2,512,512]{2,1,0:T(8,128)} collective-permute-done((f32[2,512,512]{2,1,0:T(8,128)}, f32[2,512,512]{2,1,0:T(8,128)}, u32[]{:S(2)}, u32[]{:S(2)}) %collective-permute-start) | collective-permute-done | bytes 2097184 | tf_op jit(solution)/shard_map/ppermute | solution.py:19
  67.4 4.1 add_select_fusion.7
  71.5 3.3 collective-permute-start.1
  74.7 90.2 %collective-permute-done.1 = f32[2,512,512]{2,1,0:T(8,128)} collective-permute-done((f32[2,512,512]{2,1,0:T(8,128)}, f32[2,512,512]{2,1,0:T(8,128)}, u32[]{:S(2)}, u32[]{:S(2)}) %collective-permute-start.1) | collective-permute-done | bytes 2097184 | tf_op jit(solution)/shard_map/ppermute | solution.py:19
  165.0 4.1 add_select_fusion.6
  169.0 6.2 collective-permute-start.2
  175.2 91.1 %collective-permute-done.2 = f32[2,512,512]{2,1,0:T(8,128)} collective-permute-done((f32[2,512,512]{2,1,0:T(8,128)}, f32[2,512,512]{2,1,0:T(8,128)}, u32[]{:S(2)}, u32[]{:S(2)}) %collective-permute-start.2) | collective-permute-done | bytes 2097184 | tf_op jit(solution)/shard_map/ppermute | solution.py:19
  266.4 4.1 add_select_fusion.5
  272.0 45.1 %collective-permute-done.3 = f32[2,512,512]{2,1,0:T(8,128)} collective-permute-done((f32[2,512,512]{2,1,0:T(8,128)}, f32[2,512,512]{2,1,0:T(8,128)}, u32[]{:S(2)}, u32[]{:S(2)}) %collective-permute-start.3) | collective-permute-done | bytes 2097184 | tf_op jit(solution)/shard_map/ppermute | solution.py:19
  317.1 4.1 add_select_fusion.4
  324.4 44.0 %collective-permute-done.4 = f32[2,512,512]{2,1,0:T(8,128)} collective-permute-done((f32[2,512,512]{2,1,0:T(8,128)}, f32[2,512,512]{2,1,0:T(8,128)}, u32[]{:S(2)}, u32[]{:S(2)}) %collective-permute-start.4) | collective-permute-done | bytes 2097184 | tf_op jit(solution)/shard_map/ppermute | solution.py:19
  368.4 4.1 add_select_fusion.3
  372.5 4.5 collective-permute-done.5
  377.0 4.1 add_select_fusion.2
  382.6 46.5 %collective-permute-done.6 = f32[2,512,512]{2,1,0:T(8,128)} collective-permute-done((f32[2,512,512]{2,1,0:T(8,128)}, f32[2,512,512]{2,1,0:T(8,128)}, u32[]{:S(2)}, u32[]{:S(2)}) %collective-permute-start.6) | collective-permute-done | bytes 2097184 | tf_op jit(solution)/shard_map/ppermute | solution.py:19
  429.1 4.1 add_select_fusion.1
  436.3 45.6 %collective-permute-done.7 = f32[2,512,512]{2,1,0:T(8,128)} collective-permute-done((f32[2,512,512]{2,1,0:T(8,128)}, f32[2,512,512]{2,1,0:T(8,128)}, u32[]{:S(2)}, u32[]{:S(2)}) %collective-permute-start.7) | collective-permute-done | bytes 2097184 | tf_op jit(solution)/shard_map/ppermute | solution.py:19
  481.8 4.1 add_select_fusion
  485.9 60.1 %copy.8 = f32[2,512,512]{0,2,1:T(8,128)} copy(f32[2,512,512]{2,1,0:T(8,128)} %add_select_fusion) | data formatting | bytes 4194304 | tf_op jit(solution)/shard_map/reshape | solution.py:62
  546.0 336.6 %gather_fusion = f32[8192,2]{1,0:T(8,128)} fusion(f32[2,262144]{0,1:T(8,128)} %bitcast.2, s32[8192]{0:T(1024)S(1)} %broadcast_clamp_fusion), kind=kCustom, calls=%fused_computation | custom fusion | bytes 163840 | tf_op jit(solution)/shard_map/jit(_take)/gather | solution.py:62
  882.5 7.7 multiply_bitcast_fusion
  890.3 1273.5 %reduce-scatter.2.cloned.1.call-done = f32[2,32]{0,1:T(8,128)} async-done(((f32[2,8192]{0,1:T(8,128)}), f32[2,32]{0,1:T(8,128)}) %reduce-scatter.2.cloned.1.call-update) | async-done | bytes 272 | tf_op jit(solution)/shard_map/reduce_scatter | solution.py:64
  (26 shorter events, 15.0 us)
Async XLA Ops:
  6.5 1.9 copy-start
  6.5 2157.3 %reduce-scatter.2.cloned.1.call-start = ((), (), s32[]{:S(2)}) async-start(), calls=%async_computation.1 | async-start | bytes 4210688 | tf_op jit(solution)/shard_map/reduce_scatter | solution.py:64
  6.5 2.4 copy-start.3
  21.3 46.1 %collective-permute-start = (f32[2,512,512]{2,1,0:T(8,128)}, f32[2,512,512]{2,1,0:T(8,128)}, u32[]{:S(2)}, u32[]{:S(2)}) collective-permute-start(f32[2,512,512]{2,1,0:T(8,128)} %fusion), channel_id=1, source_target_pairs={{0,1},{1,0},{2,3},{3,2},{4,5},{5,4},{6,7},{7,6},{8,9},{9,8},{10,11... | collective-permute-start | bytes 6291464 | tf_op jit(solution)/shard_map/ppermute | solution.py:19
  71.5 93.5 %collective-permute-start.1 = (f32[2,512,512]{2,1,0:T(8,128)}, f32[2,512,512]{2,1,0:T(8,128)}, u32[]{:S(2)}, u32[]{:S(2)}) collective-permute-start(f32[2,512,512]{2,1,0:T(8,128)} %add_select_fusion.7), channel_id=1, source_target_pairs={{0,2},{2,0},{1,3},{3,1},{4,6},{6,4},{5,7},{7,5},{8,10},{10,8},{9,1... | collective-permute-start | bytes 6291464 | tf_op jit(solution)/shard_map/ppermute | solution.py:19
  169.0 97.3 %collective-permute-start.2 = (f32[2,512,512]{2,1,0:T(8,128)}, f32[2,512,512]{2,1,0:T(8,128)}, u32[]{:S(2)}, u32[]{:S(2)}) collective-permute-start(f32[2,512,512]{2,1,0:T(8,128)} %add_select_fusion.6), channel_id=1, source_target_pairs={{0,4},{4,0},{1,5},{5,1},{2,6},{6,2},{3,7},{7,3},{8,12},{12,8},{9,1... | collective-permute-start | bytes 6291464 | tf_op jit(solution)/shard_map/ppermute | solution.py:19
  270.4 46.7 %collective-permute-start.3 = (f32[2,512,512]{2,1,0:T(8,128)}, f32[2,512,512]{2,1,0:T(8,128)}, u32[]{:S(2)}, u32[]{:S(2)}) collective-permute-start(f32[2,512,512]{2,1,0:T(8,128)} %add_select_fusion.5), channel_id=1, source_target_pairs={{0,8},{8,0},{1,9},{9,1},{2,10},{10,2},{3,11},{11,3},{4,12},{12,4},... | collective-permute-start | bytes 6291464 | tf_op jit(solution)/shard_map/ppermute | solution.py:19
  321.2 47.3 %collective-permute-start.4 = (f32[2,512,512]{2,1,0:T(8,128)}, f32[2,512,512]{2,1,0:T(8,128)}, u32[]{:S(2)}, u32[]{:S(2)}) collective-permute-start(f32[2,512,512]{2,1,0:T(8,128)} %add_select_fusion.4), channel_id=1, source_target_pairs={{0,16},{16,0},{1,17},{17,1},{2,18},{18,2},{3,19},{19,3},{4,20},{20... | collective-permute-start | bytes 6291464 | tf_op jit(solution)/shard_map/ppermute | solution.py:19
  372.5 4.5 collective-permute-start.5
  381.1 48.0 %collective-permute-start.6 = (f32[2,512,512]{2,1,0:T(8,128)}, f32[2,512,512]{2,1,0:T(8,128)}, u32[]{:S(2)}, u32[]{:S(2)}) collective-permute-start(f32[2,512,512]{2,1,0:T(8,128)} %add_select_fusion.2), channel_id=1, source_target_pairs={{0,64},{64,0},{32,96},{96,32},{128,192},{192,128},{160,224},{224,1... | collective-permute-start | bytes 6291464 | tf_op jit(solution)/shard_map/ppermute | solution.py:19
  382.6 53.6 %copy-start.1 = (s32[8192]{0:T(1024)S(1)}, s32[8192]{0:T(1024)}, u32[]{:S(2)}) copy-start(s32[8192]{0:T(1024)} %param.9) | copy-start | bytes 98308
  382.6 53.6 %copy-start.2 = (s32[8192]{0:T(1024)S(1)}, s32[8192]{0:T(1024)}, u32[]{:S(2)}) copy-start(s32[8192]{0:T(1024)} %param.8) | copy-start | bytes 98308
  433.1 48.7 %collective-permute-start.7 = (f32[2,512,512]{2,1,0:T(8,128)}, f32[2,512,512]{2,1,0:T(8,128)}, u32[]{:S(2)}, u32[]{:S(2)}) collective-permute-start(f32[2,512,512]{2,1,0:T(8,128)} %add_select_fusion.1), channel_id=1, source_target_pairs={{0,128},{128,0},{32,160},{160,32},{64,192},{192,64},{96,224},{224,... | collective-permute-start | bytes 6291464 | tf_op jit(solution)/shard_map/ppermute | solution.py:19
Sparse Core Ops, SparseCore 0:
  890.4 1273.3 reduce-scatter.1
where the time goes:
time: 2170 us
  waiting for transfers between devices  1690 us (78%)
  local copies, waits for them, and re-layouts  399 us (18%)
  other arithmetic  41.9 us (2%)
    reduce_scatter x1, waiting for transfers between devices, local(): lax.psum_scatter(share_term, ('grp', 'shard'), scatter_dimension=1, tiled...  1270 us
    ppermute x8, waiting for transfers between devices, partner_2(): return lax.ppermute(block, axis, route)  413 us
    gather x1, local copies, waits for them, and re-layouts, local(): jnp.take(values.reshape(examples, row_count * column_count), flat_index,...  337 us
    reshape x1, local copies, waits for them, and re-layouts, local(): values.reshape(examples, row_count * column_count)  60.1 us
  transfers between devices with their start and end apart: 9, of which 9 were waited for; matrix products, arithmetic and copies ran while one was open for 0% of the time, Pallas kernels for 0%

commit v1 on v0

v1 whole, which is shorter than its diff:
```python
import math

import jax
import jax.numpy as jnp
from jax import lax
from jax.experimental import pallas as pl
from jax.experimental.pallas import tpu as pltpu
from jax.sharding import PartitionSpec as P

F32 = jnp.float32
BF16 = jnp.bfloat16
MESH = pl.DeviceIdType.MESH

EXAMPLES = 2
TOKENS = 1024
ROWS = 512
COLS = 512
UNITS = 448
KEPT = 8192
SCALE = 1.0 / math.sqrt(4096 * 16384)
GROUP = 16
NARROW = 64
PER_ROW = 16


def parity(bits):
    for shift in (8, 4, 2, 1):
        bits = bits ^ (bits >> shift)
    return bits & 1


def hadamard(shape):
    row = lax.broadcasted_iota(jnp.int32, shape, 0)
    col = lax.broadcasted_iota(jnp.int32, shape, 1)
    return jnp.where(parity(row & col) == 1, -1.0, 1.0).astype(BF16)


def lane_transform():
    row = lax.broadcasted_iota(jnp.int32, (256, 256), 0)
    col = lax.broadcasted_iota(jnp.int32, (256, 256), 1)
    target = ((col >> 7) << 6) | (col & 63)
    sign = jnp.where(parity((row & 127) & target) == 1, -1.0, 1.0)
    return jnp.where((row >> 7) == ((col >> 6) & 1), sign, 0.0).astype(BF16)


def split(values):
    high = values.astype(BF16)
    return high, (values - high.astype(F32)).astype(BF16)


def dot(a, b):
    return jnp.dot(a, b, preferred_element_type=F32)


def kernel(
    x_hbm, c_hbm, s_hbm, row_hbm, col_hbm, out_ref,
    x_ref, c_ref, s_ref, st_ref, row_ref, col_ref, lane_ref, q_vmem, q_smem, a_ref, table,
    send1, recv1, send2, recv2,
    sems, send1_sem, recv1_sem, send2_sem, recv2_sem,
):
    grp = lax.axis_index("grp")
    shard = lax.axis_index("shard")
    own1 = grp * 2 + shard // 16
    own2 = shard % 16

    def peer1(place):
        return (place // 2, (place % 2) * 16 + own2)

    def peer2(place):
        return (grp, (shard // 16) * 16 + place)

    copies = [
        pltpu.make_async_copy(row_hbm, row_ref, sems.at[0]),
        pltpu.make_async_copy(col_hbm, col_ref, sems.at[1]),
        pltpu.make_async_copy(s_hbm, s_ref, sems.at[2]),
        pltpu.make_async_copy(x_hbm.at[0], x_ref.at[0], sems.at[3]),
        pltpu.make_async_copy(c_hbm.at[0], c_ref.at[0], sems.at[4]),
        pltpu.make_async_copy(x_hbm.at[1], x_ref.at[1], sems.at[5]),
        pltpu.make_async_copy(c_hbm.at[1], c_ref.at[1], sems.at[6]),
    ]
    for copy in copies:
        copy.start()

    barrier = pltpu.get_barrier_semaphore()

    def greet(step, carry):
        pl.semaphore_signal(barrier, inc=1, device_id=peer1((own1 + 1 + step) % GROUP), device_id_type=MESH)
        pl.semaphore_signal(barrier, inc=1, device_id=peer2((own2 + 1 + step) % GROUP), device_id_type=MESH)
        return carry

    lax.fori_loop(0, GROUP - 1, greet, 0)

    h256 = hadamard((256, 256))
    lanes = lane_transform()

    copies[0].wait()
    copies[1].wait()
    row, col = row_ref[...], col_ref[...]
    q_vmem[...] = (((row & 511) >> 6) << 9) + (col & 511)
    q_copy = pltpu.make_async_copy(q_vmem, q_smem, sems.at[7])
    q_copy.start()
    device_bits = ((row >> 9) & grp) | (((col >> 9) & shard) << 3)
    lane_ref[...] = (row & (NARROW - 1)) | (parity(device_bits) << 7)

    copies[2].wait()
    st_ref[...] = jnp.transpose(s_ref[...].astype(F32))[:UNITS]
    low_table = jnp.concatenate([h256, h256], axis=1)
    high_table = jnp.concatenate([h256[:, : UNITS - 256], h256[:, : UNITS - 256]], axis=1)
    for e in range(EXAMPLES):
        copies[3 + 2 * e].wait()
        copies[4 + 2 * e].wait()
        for n in range(2):
            part = slice(256 * n, 256 * n + 256)
            signed = dot(c_ref[e], x_ref[e, :, part]) * st_ref[:, part]
            high, low = split(signed)
            first = dot(low_table, jnp.concatenate([high[:256], low[:256]], axis=0))
            second = dot(high_table, jnp.concatenate([high[256:], low[256:]], axis=0))
            a_ref[e, :256, part] = first + second
            a_ref[e, 256:, part] = first - second
    lanes2 = jnp.concatenate([lanes, lanes], axis=0)
    for j in range(4):
        part = slice(128 * j, 128 * j + 128)
        high, low = split(jnp.concatenate([a_ref[0, :, part], a_ref[1, :, part]], axis=1))
        both = dot(jnp.concatenate([high, low], axis=1), lanes2)
        table[pl.ds(2 * j * COLS, COLS)] = both[:, :128]
        table[pl.ds((2 * j + 1) * COLS, COLS)] = both[:, 128:]
    for p in range(2):
        t = [table[pl.ds((2 * j + p) * COLS, COLS)] for j in range(4)]
        a, b, c, d = t[0] + t[1], t[0] - t[1], t[2] + t[3], t[2] - t[3]
        for j, value in enumerate((a + c, b + d, a - c, b - d)):
            table[pl.ds((2 * j + p) * COLS, COLS)] = value
    q_copy.wait()

    lane = lax.broadcasted_iota(jnp.int32, (8, 128), 1)
    sublane = lax.broadcasted_iota(jnp.int32, (8, 128), 0)
    pattern = sublane * PER_ROW
    half = lane & NARROW
    place = lane & (NARROW - 1)

    def pick(block):
        def pair(step, carry):
            found, marks = carry
            for u in range(2):
                quarter = 2 * step + u
                r = 4 * block + quarter
                source = jnp.broadcast_to(lane_ref[pl.ds(r, 1), :], (8, 128))
                here = place - quarter * PER_ROW
                for m in range(PER_ROW):
                    rows = None
                    for i in range(8):
                        q = q_smem[r, i * PER_ROW + m]
                        one = jnp.broadcast_to(table[pl.ds(q, 1), :], (8, 128))
                        rows = one if rows is None else jnp.where(sublane == i, one, rows)
                    mark = jnp.take_along_axis(source, pattern + m, axis=1, mode="promise_in_bounds")
                    index = (mark & (NARROW - 1)) | half
                    got = jnp.take_along_axis(rows, index, axis=1, mode="promise_in_bounds")
                    found = jnp.where(here == m, got, found)
                    marks = jnp.where(here == m, mark, marks)
            return found, marks

        found, marks = lax.fori_loop(0, 2, pair, (jnp.zeros((8, 128), F32), jnp.zeros((8, 128), jnp.int32)))
        return found * jnp.where(marks >= 128, -SCALE, SCALE)

    def copy1(target, source):
        return pltpu.make_async_remote_copy(
            src_ref=send1.at[target], dst_ref=recv1.at[source], send_sem=send1_sem.at[target],
            recv_sem=recv1_sem.at[source], device_id=peer1(target), device_id_type=MESH,
        )

    def copy2(target, source):
        return pltpu.make_async_remote_copy(
            src_ref=send2.at[target % 4], dst_ref=recv2.at[source], send_sem=send2_sem.at[target],
            recv_sem=recv2_sem.at[source], device_id=peer2(target), device_id_type=MESH,
        )

    pl.semaphore_wait(barrier, 2 * (GROUP - 1))

    def produce(step, carry):
        target = (own1 + 1 + step) % GROUP
        send1[target] = pick(target)
        copy1(target, own1).start()
        return carry

    lax.fori_loop(0, GROUP - 1, produce, 0)
    total = pick(own1)

    def gather1(step, total):
        source = (own1 + GROUP - 1 - step) % GROUP
        copy1(source, source).wait_recv()
        return total + recv1[source]

    total = lax.fori_loop(0, GROUP - 1, gather1, total)
    for i in range(4):
        send2[i] = total[2 * i : 2 * i + 2]

    def spread(step, carry):
        copy2((own2 + 1 + step) % GROUP, own2).start()
        return carry

    lax.fori_loop(0, GROUP - 1, spread, 0)

    def gather2(step, total):
        source = (own2 + GROUP - 1 - step) % GROUP
        copy2(source, source).wait_recv()
        return total + recv2[source]

    total = lax.fori_loop(0, GROUP - 1, gather2, send2[own2 % 4])
    quarter = (shard // 4) % 4
    total = pltpu.roll(total, (128 - quarter * PER_ROW) % 128, 1)
    for e in range(EXAMPLES):
        for i in range(2):
            out_ref[e : e + 1, PER_ROW * i : PER_ROW * i + PER_ROW] = total[i : i + 1, NARROW * e : NARROW * e + PER_ROW]

    def finish(step, carry):
        copy1((own1 + 1 + step) % GROUP, own1).wait_send()
        copy2((own2 + 1 + step) % GROUP, own2).wait_send()
        return carry

    lax.fori_loop(0, GROUP - 1, finish, 0)


def local(inputs, up_cotangent, signs, kept_row, kept_col):
    hbm = pl.BlockSpec(memory_space=pl.ANY)
    return pl.pallas_call(
        kernel,
        out_shape=jax.ShapeDtypeStruct((EXAMPLES, KEPT // 256), F32),
        in_specs=[hbm] * 5,
        out_specs=pl.BlockSpec(memory_space=pltpu.VMEM),
        scratch_shapes=[
            pltpu.VMEM((EXAMPLES, TOKENS, ROWS), BF16),
            pltpu.VMEM((EXAMPLES, UNITS, TOKENS), BF16),
            pltpu.VMEM((ROWS, COLS), jnp.int32),
            pltpu.VMEM((UNITS, ROWS), F32),
            pltpu.VMEM((64, 128), jnp.int32),
            pltpu.VMEM((64, 128), jnp.int32),
            pltpu.VMEM((64, 128), jnp.int32),
            pltpu.VMEM((64, 128), jnp.int32),
            pltpu.SMEM((64, 128), jnp.int32),
            pltpu.VMEM((EXAMPLES, COLS, ROWS), F32),
            pltpu.VMEM((8 * COLS, 128), F32),
            pltpu.VMEM((GROUP, 8, 128), F32),
            pltpu.VMEM((GROUP, 8, 128), F32),
            pltpu.VMEM((4, 2, 128), F32),
            pltpu.VMEM((GROUP, 2, 128), F32),
            pltpu.SemaphoreType.DMA((8,)),
            pltpu.SemaphoreType.DMA((GROUP,)),
            pltpu.SemaphoreType.DMA((GROUP,)),
            pltpu.SemaphoreType.DMA((GROUP,)),
            pltpu.SemaphoreType.DMA((GROUP,)),
        ],
        compiler_params=pltpu.CompilerParams(
            vmem_limit_bytes=60 << 20, collective_id=0, has_side_effects=True
        ),
    )(inputs, jnp.swapaxes(up_cotangent, 1, 2), signs, kept_row.reshape(64, 128), kept_col.reshape(64, 128))


def solution(mesh):
    placed = (P(None, None, "grp"), P(None, None, "shard"), P("grp", "shard"), P(), P())
    return jax.shard_map(
        local, mesh=mesh, in_specs=placed, out_specs=P(None, ("grp", "shard")), check_vma=False
    )
```

time: 2170 us -> 31.5 us (0.01)
  the two profiles are of different devices: /device:TPU:0 before, /device:TPU:1 now
where the time goes in v1:
time: 31.5 us; the launch traced here: 31.1 us
  Pallas kernels  29.9 us (95%)
  local copies, waits for them, and re-layouts  1.24 us (4%)
    pallas_call x1, Pallas kernels, local(): pl.pallas_call(kernel, out_shape=jax.ShapeDtypeStruct((EXAMPLES, KEPT //...  29.9 us
    unnamed x1, local copies, waits for them, and re-layouts  1.24 us

profile of v1, /device:TPU:1, one launch (start us, length us, event | category | flops | bytes accessed | tf_op | source)
XLA Modules:
  0.0 31.1 jit_solution(5915060522713929978)
XLA Ops:
  0.0 29.9 %shard_map.55 = f32[2,32]{1,0:T(2,128)} custom-call(bf16[2,1024,512]{2,1,0:T(8,128)(2,1)} %x_hbm.1, bf16[2,448,1024]{2,1,0:T(8,128)(2,1)} %bitcast.3, s32[512,512]{1,0:T(8,128)} %s_hbm.1, s32[64,128]{1,0:T(8,128)} %bitcast.4, s32[64,128]{1,0:T(8,128)} %bitcast.5), custom_call_target="tpu_custom_call" | custom-call | tf_op jit(solution)/shard_map/pallas_call | solution.py:224
  29.9 1.2 %copy.7 = f32[2,32]{1,0:T(2,128)} copy(f32[2,32]{1,0:T(2,128)} %shard_map.55) | data formatting | bytes 512

commit v2 on v1

--- a/solution.py
+++ b/solution.py
@@ -48,13 +48,27 @@
     return high, (values - high.astype(F32)).astype(BF16)
 
 
+def permute(values, index):
+    numbers = lax.GatherDimensionNumbers(
+        offset_dims=(), collapsed_slice_dims=(1,), start_index_map=(1,),
+        operand_batching_dims=(0,), start_indices_batching_dims=(0,),
+    )
+    return lax.gather(values, index[..., None], numbers, (1, 1), mode=lax.GatherScatterMode.PROMISE_IN_BOUNDS)
+
+
+def spread_table(columns, chosen):
+    row = lax.broadcasted_iota(jnp.int32, (128, columns), 0)
+    col = lax.broadcasted_iota(jnp.int32, (128, columns), 1)
+    return jnp.where((row & (PER_ROW - 1)) == chosen(col), 1.0, 0.0).astype(BF16)
+
+
 def dot(a, b):
     return jnp.dot(a, b, preferred_element_type=F32)
 
 
 def kernel(
     x_hbm, c_hbm, s_hbm, row_hbm, col_hbm, out_ref,
-    x_ref, c_ref, s_ref, st_ref, row_ref, col_ref, lane_ref, q_vmem, q_smem, a_ref, table,
+    x_ref, c_ref, s_ref, st_ref, row_ref, col_ref, q_vmem, q_smem, index_ref, sign_ref, split_ref, table,
     send1, recv1, send2, recv2,
     sems, send1_sem, recv1_sem, send2_sem, recv2_sem,
 ):
@@ -99,8 +113,30 @@
     q_vmem[...] = (((row & 511) >> 6) << 9) + (col & 511)
     q_copy = pltpu.make_async_copy(q_vmem, q_smem, sems.at[7])
     q_copy.start()
+    lane = lax.broadcasted_iota(jnp.int32, (8, 128), 1)
+    sublane = lax.broadcasted_iota(jnp.int32, (8, 128), 0)
     device_bits = ((row >> 9) & grp) | (((col >> 9) & shard) << 3)
-    lane_ref[...] = (row & (NARROW - 1)) | (parity(device_bits) << 7)
+    sign = jnp.where(parity(device_bits) == 1, -1.0, 1.0)
+    inner = (row & (NARROW - 1)).astype(F32)
+    mine = (lane // PER_ROW) == sublane
+
+    def diagonal(values):
+        blocks = [jnp.where(mine, jnp.broadcast_to(values[r : r + 1], (8, 128)), 0.0) for r in range(64)]
+        return jnp.concatenate(blocks, axis=0).astype(BF16)
+
+    spots = diagonal(inner)
+    for pair in range(PER_ROW // 2):
+        found = dot(spots, spread_table(256, lambda y: 2 * pair + (y >> 7))).astype(jnp.int32)
+        for u in range(2):
+            part = found[:, 128 * u : 128 * u + 128].reshape(64, 8, 128)
+            index_ref[:, 2 * pair + u] = part + (lane & NARROW)[None]
+    found = dot(diagonal(sign), spread_table(128, lambda y: y & (PER_ROW - 1))) * SCALE
+    for b in range(GROUP):
+        value = found[32 * b : 32 * b + 8]
+        for quarter in range(1, 4):
+            here = ((lane // PER_ROW) & 3) == quarter
+            value = jnp.where(here, found[32 * b + 8 * quarter : 32 * b + 8 * quarter + 8], value)
+        sign_ref[b] = value
 
     copies[2].wait()
     st_ref[...] = jnp.transpose(s_ref[...].astype(F32))[:UNITS]
@@ -109,57 +145,41 @@
     for e in range(EXAMPLES):
         copies[3 + 2 * e].wait()
         copies[4 + 2 * e].wait()
-        for n in range(2):
-            part = slice(256 * n, 256 * n + 256)
-            signed = dot(c_ref[e], x_ref[e, :, part]) * st_ref[:, part]
-            high, low = split(signed)
-            first = dot(low_table, jnp.concatenate([high[:256], low[:256]], axis=0))
-            second = dot(high_table, jnp.concatenate([high[256:], low[256:]], axis=0))
-            a_ref[e, :256, part] = first + second
-            a_ref[e, 256:, part] = first - second
+        signed = dot(c_ref[e], x_ref[e]) * st_ref[...]
+        t = [signed[:, 128 * j : 128 * j + 128] for j in range(4)]
+        a, b, c, d = t[0] + t[1], t[0] - t[1], t[2] + t[3], t[2] - t[3]
+        part = slice(128 * e, 128 * e + 128)
+        for j, value in enumerate((a + c, b + d, a - c, b - d)):
+            high, low = split(value)
+            split_ref[j, :256, part] = high[:256]
+            split_ref[j, 256:512, part] = low[:256]
+            split_ref[j, 512 : 256 + UNITS, part] = high[256:]
+            split_ref[j, 256 + UNITS :, part] = low[256:]
     lanes2 = jnp.concatenate([lanes, lanes], axis=0)
     for j in range(4):
-        part = slice(128 * j, 128 * j + 128)
-        high, low = split(jnp.concatenate([a_ref[0, :, part], a_ref[1, :, part]], axis=1))
-        both = dot(jnp.concatenate([high, low], axis=1), lanes2)
-        table[pl.ds(2 * j * COLS, COLS)] = both[:, :128]
-        table[pl.ds((2 * j + 1) * COLS, COLS)] = both[:, 128:]
-    for p in range(2):
-        t = [table[pl.ds((2 * j + p) * COLS, COLS)] for j in range(4)]
-        a, b, c, d = t[0] + t[1], t[0] - t[1], t[2] + t[3], t[2] - t[3]
-        for j, value in enumerate((a + c, b + d, a - c, b - d)):
-            table[pl.ds((2 * j + p) * COLS, COLS)] = value
+        first = dot(low_table, split_ref[j, :512])
+        second = dot(high_table, split_ref[j, 512:])
+        for upper, value in enumerate((first + second, first - second)):
+            high, low = split(value)
+            both = dot(jnp.concatenate([high, low], axis=1), lanes2)
+            table[pl.ds(2 * j * COLS + 256 * upper, 256)] = both[:, :128]
+            table[pl.ds((2 * j + 1) * COLS + 256 * upper, 256)] = both[:, 128:]
     q_copy.wait()
 
-    lane = lax.broadcasted_iota(jnp.int32, (8, 128), 1)
-    sublane = lax.broadcasted_iota(jnp.int32, (8, 128), 0)
-    pattern = sublane * PER_ROW
-    half = lane & NARROW
     place = lane & (NARROW - 1)
 
     def pick(block):
-        def pair(step, carry):
-            found, marks = carry
-            for u in range(2):
-                quarter = 2 * step + u
-                r = 4 * block + quarter
-                source = jnp.broadcast_to(lane_ref[pl.ds(r, 1), :], (8, 128))
-                here = place - quarter * PER_ROW
-                for m in range(PER_ROW):
-                    rows = None
-                    for i in range(8):
-                        q = q_smem[r, i * PER_ROW + m]
-                        one = jnp.broadcast_to(table[pl.ds(q, 1), :], (8, 128))
-                        rows = one if rows is None else jnp.where(sublane == i, one, rows)
-                    mark = jnp.take_along_axis(source, pattern + m, axis=1, mode="promise_in_bounds")
-                    index = (mark & (NARROW - 1)) | half
-                    got = jnp.take_along_axis(rows, index, axis=1, mode="promise_in_bounds")
-                    found = jnp.where(here == m, got, found)
-                    marks = jnp.where(here == m, mark, marks)
-            return found, marks
-
-        found, marks = lax.fori_loop(0, 2, pair, (jnp.zeros((8, 128), F32), jnp.zeros((8, 128), jnp.int32)))
-        return found * jnp.where(marks >= 128, -SCALE, SCALE)
+        found = jnp.zeros((8, 128), F32)
+        for quarter in range(4):
+            r = 4 * block + quarter
+            for m in range(PER_ROW):
+                rows = None
+                for i in range(8):
+                    q = q_smem.at[:, pl.ds(i * PER_ROW + m, 1)][r, 0]
+                    one = jnp.broadcast_to(table[pl.ds(q, 1), :], (8, 128))
+                    rows = one if rows is None else jnp.where(sublane == i, one, rows)
+                found = jnp.where(place == quarter * PER_ROW + m, permute(rows, index_ref[r, m]), found)
+        return found * sign_ref[block]
 
     def copy1(target, source):
         return pltpu.make_async_remote_copy(
@@ -178,18 +198,21 @@
     def produce(step, carry):
         target = (own1 + 1 + step) % GROUP
         send1[target] = pick(target)
-        copy1(target, own1).start()
-        return carry
-
-    lax.fori_loop(0, GROUP - 1, produce, 0)
-    total = pick(own1)
+
+        @pl.when(step < GROUP - 1)
+        def _():
+            copy1(target, own1).start()
+
+        return carry
+
+    lax.fori_loop(0, GROUP, produce, 0)
 
     def gather1(step, total):
         source = (own1 + GROUP - 1 - step) % GROUP
         copy1(source, source).wait_recv()
         return total + recv1[source]
 
-    total = lax.fori_loop(0, GROUP - 1, gather1, total)
+    total = lax.fori_loop(0, GROUP - 1, gather1, send1[own1])
     for i in range(4):
         send2[i] = total[2 * i : 2 * i + 2]
 
@@ -234,9 +257,10 @@
             pltpu.VMEM((64, 128), jnp.int32),
             pltpu.VMEM((64, 128), jnp.int32),
             pltpu.VMEM((64, 128), jnp.int32),
-            pltpu.VMEM((64, 128), jnp.int32),
             pltpu.SMEM((64, 128), jnp.int32),
-            pltpu.VMEM((EXAMPLES, COLS, ROWS), F32),
+            pltpu.VMEM((64, PER_ROW, 8, 128), jnp.int32),
+            pltpu.VMEM((GROUP, 8, 128), F32),
+            pltpu.VMEM((4, 2 * UNITS, 256), BF16),
             pltpu.VMEM((8 * COLS, 128), F32),
             pltpu.VMEM((GROUP, 8, 128), F32),
             pltpu.VMEM((GROUP, 8, 128), F32),
@@ -249,7 +273,7 @@
             pltpu.SemaphoreType.DMA((GROUP,)),
         ],
         compiler_params=pltpu.CompilerParams(
-            vmem_limit_bytes=60 << 20, collective_id=0, has_side_effects=True
+            vmem_limit_bytes=64 << 20, collective_id=0, has_side_effects=True
         ),
     )(inputs, jnp.swapaxes(up_cotangent, 1, 2), signs, kept_row.reshape(64, 128), kept_col.reshape(64, 128))
 

time: 31.5 us -> 27.5 us (0.87)
  Pallas kernels: 29.9 us -> 26.1 us
    pallas_call x1, Pallas kernels: 29.9 us -> 26.1 us  [local(): pl.pallas_call(kernel, out_shape=jax.ShapeDtypeStruct((EXAMPLES, KEPT //...]
where the time goes in v2:
time: 27.5 us; the launch traced here: 27.4 us
  Pallas kernels  26.1 us (95%)
  local copies, waits for them, and re-layouts  1.24 us (5%)
    pallas_call x1, Pallas kernels, local(): pl.pallas_call(kernel, out_shape=jax.ShapeDtypeStruct((EXAMPLES, KEPT //...  26.1 us
    unnamed x1, local copies, waits for them, and re-layouts  1.24 us

profile of v2, /device:TPU:1, one launch (start us, length us, event | category | flops | bytes accessed | tf_op | source)
XLA Modules:
  0.0 27.4 jit_solution(11218673563805821107)
XLA Ops:
  0.0 26.1 %shard_map.55 = f32[2,32]{1,0:T(2,128)} custom-call(bf16[2,1024,512]{2,1,0:T(8,128)(2,1)} %x_hbm.1, bf16[2,448,1024]{2,1,0:T(8,128)(2,1)} %bitcast.3, s32[512,512]{1,0:T(8,128)} %s_hbm.1, s32[64,128]{1,0:T(8,128)} %bitcast.4, s32[64,128]{1,0:T(8,128)} %bitcast.5), custom_call_target="tpu_custom_call" | custom-call | tf_op jit(solution)/shard_map/pallas_call | solution.py:247
  26.1 1.2 %copy.7 = f32[2,32]{1,0:T(2,128)} copy(f32[2,32]{1,0:T(2,128)} %shard_map.55) | data formatting | bytes 512

commit v3 on v2

--- a/solution.py
+++ b/solution.py
@@ -18,7 +18,8 @@
 UNITS = 448
 KEPT = 8192
 SCALE = 1.0 / math.sqrt(4096 * 16384)
-GROUP = 16
+FIRST = 32
+SECOND = 8
 NARROW = 64
 PER_ROW = 16
 
@@ -64,6 +65,28 @@
 
 def dot(a, b):
     return jnp.dot(a, b, preferred_element_type=F32)
+
+
+def hops(offset, length):
+    return min(offset, length - offset)
+
+
+def pack(order, width):
+    words = [sum(order[6 * w + n] << (width * n) for n in range(6) if 6 * w + n < len(order)) for w in range((len(order) + 5) // 6)]
+
+    def read(step):
+        word = words[-1]
+        for w in range(len(words) - 2, -1, -1):
+            word = jnp.where(step // 6 == w, words[w], word)
+        return (word >> (width * (step % 6))) & ((1 << width) - 1)
+
+    return read
+
+
+first_order = sorted(range(FIRST), key=lambda c: -hops(c // 8, 4) - hops(c % 8, 8))
+second_order = sorted(range(SECOND), key=lambda c: (-hops(c // 2, 4), -(c % 2)))
+first_offset = pack(first_order, 5)
+second_offset = pack(second_order, 3)
 
 
 def kernel(
@@ -74,14 +97,17 @@
 ):
     grp = lax.axis_index("grp")
     shard = lax.axis_index("shard")
-    own1 = grp * 2 + shard // 16
-    own2 = shard % 16
-
-    def peer1(place):
-        return (place // 2, (place % 2) * 16 + own2)
-
-    def peer2(place):
-        return (grp, (shard // 16) * 16 + place)
+
+    def peer1(step, sign):
+        code = first_offset(step)
+        y = (shard // 8 + 4 + sign * (code // 8)) % 4
+        z = (shard % 8 + 8 + sign * (code % 8)) % 8
+        return y * 8 + z
+
+    def peer2(step, sign):
+        code = second_offset(step)
+        x = (grp // 2 + 4 + sign * (code // 2)) % 4
+        return x * 2 + (grp + code) % 2
 
     copies = [
         pltpu.make_async_copy(row_hbm, row_ref, sems.at[0]),
@@ -97,12 +123,16 @@
 
     barrier = pltpu.get_barrier_semaphore()
 
-    def greet(step, carry):
-        pl.semaphore_signal(barrier, inc=1, device_id=peer1((own1 + 1 + step) % GROUP), device_id_type=MESH)
-        pl.semaphore_signal(barrier, inc=1, device_id=peer2((own2 + 1 + step) % GROUP), device_id_type=MESH)
+    def greet1(step, carry):
+        pl.semaphore_signal(barrier, inc=1, device_id=(grp, peer1(step, -1)), device_id_type=MESH)
         return carry
 
-    lax.fori_loop(0, GROUP - 1, greet, 0)
+    def greet2(step, carry):
+        pl.semaphore_signal(barrier, inc=1, device_id=(peer2(step, -1), shard), device_id_type=MESH)
+        return carry
+
+    lax.fori_loop(0, FIRST - 1, greet1, 0)
+    lax.fori_loop(0, SECOND - 1, greet2, 0)
 
     h256 = hadamard((256, 256))
     lanes = lane_transform()
@@ -110,14 +140,27 @@
     copies[0].wait()
     copies[1].wait()
     row, col = row_ref[...], col_ref[...]
-    q_vmem[...] = (((row & 511) >> 6) << 9) + (col & 511)
+    device_bits = ((row >> 9) & grp) | (((col >> 9) & shard) << 3)
+    entry = ((row & 511) >> 6) * COLS + (col & 511)
+    packed = entry | ((row & (NARROW - 1)) << 12) | (parity(device_bits) << 18)
+    lane = lax.broadcasted_iota(jnp.int32, (8, 128), 1)
+    sublane = lax.broadcasted_iota(jnp.int32, (8, 128), 0)
+    ordered = []
+    for chunk in range(8):
+        at = (chunk % 4) * 2 + chunk // 4
+        value = None
+        for i in range(SECOND):
+            moved = packed[8 * i : 8 * i + 8]
+            if i != at:
+                moved = pltpu.roll(moved, ((i - at) % 8) * PER_ROW, 1)
+            value = moved if value is None else jnp.where(lane // PER_ROW == i, moved, value)
+        ordered.append(value)
+    packed = jnp.concatenate(ordered, axis=0)
+    q_vmem[...] = packed & 4095
     q_copy = pltpu.make_async_copy(q_vmem, q_smem, sems.at[7])
     q_copy.start()
-    lane = lax.broadcasted_iota(jnp.int32, (8, 128), 1)
-    sublane = lax.broadcasted_iota(jnp.int32, (8, 128), 0)
-    device_bits = ((row >> 9) & grp) | (((col >> 9) & shard) << 3)
-    sign = jnp.where(parity(device_bits) == 1, -1.0, 1.0)
-    inner = (row & (NARROW - 1)).astype(F32)
+    sign = jnp.where((packed >> 18) == 1, -1.0, 1.0)
+    inner = ((packed >> 12) & (NARROW - 1)).astype(F32)
     mine = (lane // PER_ROW) == sublane
 
     def diagonal(values):
@@ -131,12 +174,9 @@
             part = found[:, 128 * u : 128 * u + 128].reshape(64, 8, 128)
             index_ref[:, 2 * pair + u] = part + (lane & NARROW)[None]
     found = dot(diagonal(sign), spread_table(128, lambda y: y & (PER_ROW - 1))) * SCALE
-    for b in range(GROUP):
-        value = found[32 * b : 32 * b + 8]
-        for quarter in range(1, 4):
-            here = ((lane // PER_ROW) & 3) == quarter
-            value = jnp.where(here, found[32 * b + 8 * quarter : 32 * b + 8 * quarter + 8], value)
-        sign_ref[b] = value
+    for r in range(FIRST):
+        second_half = found[8 * (FIRST + r) : 8 * (FIRST + r) + 8]
+        sign_ref[r] = jnp.where((lane // PER_ROW) % 2 == 1, second_half, found[8 * r : 8 * r + 8])
 
     copies[2].wait()
     st_ref[...] = jnp.transpose(s_ref[...].astype(F32))[:UNITS]
@@ -168,78 +208,57 @@
 
     place = lane & (NARROW - 1)
 
-    def pick(block):
+    def pick(target):
+        block = (target % 4) * 8 + target // 4
         found = jnp.zeros((8, 128), F32)
-        for quarter in range(4):
-            r = 4 * block + quarter
+        for half in range(2):
+            r = block + half * FIRST
             for m in range(PER_ROW):
                 rows = None
-                for i in range(8):
+                for i in range(SECOND):
                     q = q_smem.at[:, pl.ds(i * PER_ROW + m, 1)][r, 0]
                     one = jnp.broadcast_to(table[pl.ds(q, 1), :], (8, 128))
                     rows = one if rows is None else jnp.where(sublane == i, one, rows)
-                found = jnp.where(place == quarter * PER_ROW + m, permute(rows, index_ref[r, m]), found)
+                found = jnp.where(place == half * PER_ROW + m, permute(rows, index_ref[r, m]), found)
         return found * sign_ref[block]
 
-    def copy1(target, source):
-        return pltpu.make_async_remote_copy(
-            src_ref=send1.at[target], dst_ref=recv1.at[source], send_sem=send1_sem.at[target],
-            recv_sem=recv1_sem.at[source], device_id=peer1(target), device_id_type=MESH,
-        )
-
-    def copy2(target, source):
-        return pltpu.make_async_remote_copy(
-            src_ref=send2.at[target % 4], dst_ref=recv2.at[source], send_sem=send2_sem.at[target],
-            recv_sem=recv2_sem.at[source], device_id=peer2(target), device_id_type=MESH,
-        )
-
-    pl.semaphore_wait(barrier, 2 * (GROUP - 1))
+    pl.semaphore_wait(barrier, FIRST + SECOND - 2)
 
     def produce(step, carry):
-        target = (own1 + 1 + step) % GROUP
-        send1[target] = pick(target)
-
-        @pl.when(step < GROUP - 1)
+        target = peer1(step, 1)
+        send1[step] = pick(target)
+
+        @pl.when(step < FIRST - 1)
         def _():
-            copy1(target, own1).start()
+            pltpu.make_async_remote_copy(
+                src_ref=send1.at[step], dst_ref=recv1.at[step], send_sem=send1_sem, recv_sem=recv1_sem,
+                device_id=(grp, target), device_id_type=MESH,
+            ).start()
 
         return carry
 
-    lax.fori_loop(0, GROUP, produce, 0)
-
-    def gather1(step, total):
-        source = (own1 + GROUP - 1 - step) % GROUP
-        copy1(source, source).wait_recv()
-        return total + recv1[source]
-
-    total = lax.fori_loop(0, GROUP - 1, gather1, send1[own1])
-    for i in range(4):
-        send2[i] = total[2 * i : 2 * i + 2]
-
-    def spread(step, carry):
-        copy2((own2 + 1 + step) % GROUP, own2).start()
-        return carry
-
-    lax.fori_loop(0, GROUP - 1, spread, 0)
-
-    def gather2(step, total):
-        source = (own2 + GROUP - 1 - step) % GROUP
-        copy2(source, source).wait_recv()
-        return total + recv2[source]
-
-    total = lax.fori_loop(0, GROUP - 1, gather2, send2[own2 % 4])
-    quarter = (shard // 4) % 4
-    total = pltpu.roll(total, (128 - quarter * PER_ROW) % 128, 1)
+    lax.fori_loop(0, FIRST, produce, 0)
+    pltpu.make_async_copy(recv1, recv1, recv1_sem).wait()
+    total = send1[FIRST - 1]
+    for step in range(FIRST - 1):
+        total = total + recv1[step]
+    for g in range(SECOND):
+        send2[g] = total[g : g + 1]
+    for step in range(SECOND - 1):
+        target = peer2(step, 1)
+        pltpu.make_async_remote_copy(
+            src_ref=send2.at[target], dst_ref=recv2.at[step], send_sem=send2_sem, recv_sem=recv2_sem,
+            device_id=(target, shard), device_id_type=MESH,
+        ).start()
+    sent = send1.at[pl.ds(0, FIRST - 1)]
+    pltpu.make_async_copy(sent, sent, send1_sem).wait()
+    total = send2[grp]
+    pltpu.make_async_copy(recv2, recv2, recv2_sem).wait()
+    for step in range(SECOND - 1):
+        total = total + recv2[step]
     for e in range(EXAMPLES):
-        for i in range(2):
-            out_ref[e : e + 1, PER_ROW * i : PER_ROW * i + PER_ROW] = total[i : i + 1, NARROW * e : NARROW * e + PER_ROW]
-
-    def finish(step, carry):
-        copy1((own1 + 1 + step) % GROUP, own1).wait_send()
-        copy2((own2 + 1 + step) % GROUP, own2).wait_send()
-        return carry
-
-    lax.fori_loop(0, GROUP - 1, finish, 0)
+        out_ref[e : e + 1, :] = total[:, NARROW * e : NARROW * e + KEPT // 256]
+    pltpu.make_async_copy(recv2, recv2, send2_sem).wait()
 
 
 def local(inputs, up_cotangent, signs, kept_row, kept_col):
@@ -259,18 +278,18 @@
             pltpu.VMEM((64, 128), jnp.int32),
             pltpu.SMEM((64, 128), jnp.int32),
             pltpu.VMEM((64, PER_ROW, 8, 128), jnp.int32),
-            pltpu.VMEM((GROUP, 8, 128), F32),
+            pltpu.VMEM((FIRST, 8, 128), F32),
             pltpu.VMEM((4, 2 * UNITS, 256), BF16),
             pltpu.VMEM((8 * COLS, 128), F32),
-            pltpu.VMEM((GROUP, 8, 128), F32),
-            pltpu.VMEM((GROUP, 8, 128), F32),
-            pltpu.VMEM((4, 2, 128), F32),
-            pltpu.VMEM((GROUP, 2, 128), F32),
+            pltpu.VMEM((FIRST, 8, 128), F32),
+            pltpu.VMEM((FIRST - 1, 8, 128), F32),
+            pltpu.VMEM((SECOND, 1, 128), F32),
+            pltpu.VMEM((SECOND - 1, 1, 128), F32),
             pltpu.SemaphoreType.DMA((8,)),
-            pltpu.SemaphoreType.DMA((GROUP,)),
-            pltpu.SemaphoreType.DMA((GROUP,)),
-            pltpu.SemaphoreType.DMA((GROUP,)),
-            pltpu.SemaphoreType.DMA((GROUP,)),
+            pltpu.SemaphoreType.DMA,
+            pltpu.SemaphoreType.DMA,
+            pltpu.SemaphoreType.DMA,
+            pltpu.SemaphoreType.DMA,
         ],
         compiler_params=pltpu.CompilerParams(
             vmem_limit_bytes=64 << 20, collective_id=0, has_side_effects=True

time: 27.5 us -> 28.6 us (1.040)
  Pallas kernels: 26.1 us -> 27.3 us
    pallas_call x1, Pallas kernels: 26.1 us -> 27.3 us  [local(): pl.pallas_call(kernel, out_shape=jax.ShapeDtypeStruct((EXAMPLES, KEPT //...]
where the time goes in v3:
time: 28.6 us
  Pallas kernels  27.3 us (95%)
  local copies, waits for them, and re-layouts  1.24 us (4%)
    pallas_call x1, Pallas kernels, local(): pl.pallas_call(kernel, out_shape=jax.ShapeDtypeStruct((EXAMPLES, KEPT //...  27.3 us
    unnamed x1, local copies, waits for them, and re-layouts  1.24 us

profile of v3, /device:TPU:1, one launch (start us, length us, event | category | flops | bytes accessed | tf_op | source)
XLA Modules:
  0.0 28.6 jit_solution(15185463030434635411)
XLA Ops:
  0.0 27.3 %shard_map.55 = f32[2,32]{1,0:T(2,128)} custom-call(bf16[2,1024,512]{2,1,0:T(8,128)(2,1)} %x_hbm.1, bf16[2,448,1024]{2,1,0:T(8,128)(2,1)} %bitcast.3, s32[512,512]{1,0:T(8,128)} %s_hbm.1, s32[64,128]{1,0:T(8,128)} %bitcast.4, s32[64,128]{1,0:T(8,128)} %bitcast.5), custom_call_target="tpu_custom_call" | custom-call | tf_op jit(solution)/shard_map/pallas_call | solution.py:266
  27.3 1.2 %copy.7 = f32[2,32]{1,0:T(2,128)} copy(f32[2,32]{1,0:T(2,128)} %shard_map.55) | data formatting | bytes 512

commit v4 on v3

--- a/solution.py
+++ b/solution.py
@@ -71,22 +71,21 @@
     return min(offset, length - offset)
 
 
-def pack(order, width):
-    words = [sum(order[6 * w + n] << (width * n) for n in range(6) if 6 * w + n < len(order)) for w in range((len(order) + 5) // 6)]
+def pack(order):
+    words = [sum(code << (8 * n) for n, code in enumerate(order[w : w + 4])) for w in range(0, len(order), 4)]
 
     def read(step):
         word = words[-1]
         for w in range(len(words) - 2, -1, -1):
-            word = jnp.where(step // 6 == w, words[w], word)
-        return (word >> (width * (step % 6))) & ((1 << width) - 1)
+            word = jnp.where((step >> 2) == w, words[w], word)
+        return (word >> ((step & 3) * 8)) & 31
 
     return read
 
 
 first_order = sorted(range(FIRST), key=lambda c: -hops(c // 8, 4) - hops(c % 8, 8))
 second_order = sorted(range(SECOND), key=lambda c: (-hops(c // 2, 4), -(c % 2)))
-first_offset = pack(first_order, 5)
-second_offset = pack(second_order, 3)
+first_offset = pack(first_order)
 
 
 def kernel(
@@ -98,16 +97,13 @@
     grp = lax.axis_index("grp")
     shard = lax.axis_index("shard")
 
-    def peer1(step, sign):
+    def peer1(step):
         code = first_offset(step)
-        y = (shard // 8 + 4 + sign * (code // 8)) % 4
-        z = (shard % 8 + 8 + sign * (code % 8)) % 8
-        return y * 8 + z
-
-    def peer2(step, sign):
-        code = second_offset(step)
-        x = (grp // 2 + 4 + sign * (code // 2)) % 4
-        return x * 2 + (grp + code) % 2
+        return ((shard + (code & 24)) & 24) | ((shard + code) & 7)
+
+    def peer2(step):
+        code = second_order[step]
+        return ((grp + (code & 6)) & 6) | ((grp ^ code) & 1)
 
     copies = [
         pltpu.make_async_copy(row_hbm, row_ref, sems.at[0]),
@@ -123,16 +119,13 @@
 
     barrier = pltpu.get_barrier_semaphore()
 
-    def greet1(step, carry):
-        pl.semaphore_signal(barrier, inc=1, device_id=(grp, peer1(step, -1)), device_id_type=MESH)
+    def greet(step, carry):
+        pl.semaphore_signal(barrier, inc=1, device_id=(grp, shard ^ step), device_id_type=MESH)
         return carry
 
-    def greet2(step, carry):
-        pl.semaphore_signal(barrier, inc=1, device_id=(peer2(step, -1), shard), device_id_type=MESH)
-        return carry
-
-    lax.fori_loop(0, FIRST - 1, greet1, 0)
-    lax.fori_loop(0, SECOND - 1, greet2, 0)
+    lax.fori_loop(1, FIRST, greet, 0)
+    for step in range(1, SECOND):
+        pl.semaphore_signal(barrier, inc=1, device_id=(grp ^ step, shard), device_id_type=MESH)
 
     h256 = hadamard((256, 256))
     lanes = lane_transform()
@@ -209,7 +202,7 @@
     place = lane & (NARROW - 1)
 
     def pick(target):
-        block = (target % 4) * 8 + target // 4
+        block = ((target & 3) << 3) | (target >> 2)
         found = jnp.zeros((8, 128), F32)
         for half in range(2):
             r = block + half * FIRST
@@ -224,20 +217,25 @@
 
     pl.semaphore_wait(barrier, FIRST + SECOND - 2)
 
-    def produce(step, carry):
-        target = peer1(step, 1)
-        send1[step] = pick(target)
-
-        @pl.when(step < FIRST - 1)
+    def send(step, target):
+        pltpu.make_async_remote_copy(
+            src_ref=send1.at[step], dst_ref=recv1.at[step], send_sem=send1_sem, recv_sem=recv1_sem,
+            device_id=(grp, target), device_id_type=MESH,
+        ).start()
+
+    def produce(pair, targets):
+        first, second = 2 * pair, 2 * pair + 1
+        found = pick(targets[0]), pick(targets[1])
+        send1[first], send1[second] = found
+        send(first, targets[0])
+
+        @pl.when(second < FIRST - 1)
         def _():
-            pltpu.make_async_remote_copy(
-                src_ref=send1.at[step], dst_ref=recv1.at[step], send_sem=send1_sem, recv_sem=recv1_sem,
-                device_id=(grp, target), device_id_type=MESH,
-            ).start()
-
-        return carry
-
-    lax.fori_loop(0, FIRST, produce, 0)
+            send(second, targets[1])
+
+        return peer1(first + 2), peer1(second + 2)
+
+    lax.fori_loop(0, FIRST // 2, produce, (peer1(0), peer1(1)))
     pltpu.make_async_copy(recv1, recv1, recv1_sem).wait()
     total = send1[FIRST - 1]
     for step in range(FIRST - 1):
@@ -245,7 +243,7 @@
     for g in range(SECOND):
         send2[g] = total[g : g + 1]
     for step in range(SECOND - 1):
-        target = peer2(step, 1)
+        target = peer2(step)
         pltpu.make_async_remote_copy(
             src_ref=send2.at[target], dst_ref=recv2.at[step], send_sem=send2_sem, recv_sem=recv2_sem,
             device_id=(target, shard), device_id_type=MESH,

time: 28.6 us -> 26.9 us (0.941)
  Pallas kernels: 27.3 us -> 25.6 us
    pallas_call x1, Pallas kernels: 27.3 us -> 25.6 us  [local(): pl.pallas_call(kernel, out_shape=jax.ShapeDtypeStruct((EXAMPLES, KEPT //...]
where the time goes in v4:
time: 26.9 us; the launch traced here: 26.8 us
  Pallas kernels  25.6 us (95%)
  local copies, waits for them, and re-layouts  1.24 us (5%)
    pallas_call x1, Pallas kernels, local(): pl.pallas_call(kernel, out_shape=jax.ShapeDtypeStruct((EXAMPLES, KEPT //...  25.6 us
    unnamed x1, local copies, waits for them, and re-layouts  1.24 us

profile of v4, /device:TPU:1, one launch (start us, length us, event | category | flops | bytes accessed | tf_op | source)
XLA Modules:
  0.0 26.8 jit_solution(107013851638442959)
XLA Ops:
  0.0 25.6 %shard_map.55 = f32[2,32]{1,0:T(2,128)} custom-call(bf16[2,1024,512]{2,1,0:T(8,128)(2,1)} %x_hbm.1, bf16[2,448,1024]{2,1,0:T(8,128)(2,1)} %bitcast.3, s32[512,512]{1,0:T(8,128)} %s_hbm.1, s32[64,128]{1,0:T(8,128)} %bitcast.4, s32[64,128]{1,0:T(8,128)} %bitcast.5), custom_call_target="tpu_custom_call" | custom-call | tf_op jit(solution)/shard_map/pallas_call | solution.py:264
  25.6 1.2 %copy.7 = f32[2,32]{1,0:T(2,128)} copy(f32[2,32]{1,0:T(2,128)} %shard_map.55) | data formatting | bytes 512

commit v5 on v4

--- a/solution.py
+++ b/solution.py
@@ -67,27 +67,6 @@
     return jnp.dot(a, b, preferred_element_type=F32)
 
 
-def hops(offset, length):
-    return min(offset, length - offset)
-
-
-def pack(order):
-    words = [sum(code << (8 * n) for n, code in enumerate(order[w : w + 4])) for w in range(0, len(order), 4)]
-
-    def read(step):
-        word = words[-1]
-        for w in range(len(words) - 2, -1, -1):
-            word = jnp.where((step >> 2) == w, words[w], word)
-        return (word >> ((step & 3) * 8)) & 31
-
-    return read
-
-
-first_order = sorted(range(FIRST), key=lambda c: -hops(c // 8, 4) - hops(c % 8, 8))
-second_order = sorted(range(SECOND), key=lambda c: (-hops(c // 2, 4), -(c % 2)))
-first_offset = pack(first_order)
-
-
 def kernel(
     x_hbm, c_hbm, s_hbm, row_hbm, col_hbm, out_ref,
     x_ref, c_ref, s_ref, st_ref, row_ref, col_ref, q_vmem, q_smem, index_ref, sign_ref, split_ref, table,
@@ -98,12 +77,7 @@
     shard = lax.axis_index("shard")
 
     def peer1(step):
-        code = first_offset(step)
-        return ((shard + (code & 24)) & 24) | ((shard + code) & 7)
-
-    def peer2(step):
-        code = second_order[step]
-        return ((grp + (code & 6)) & 6) | ((grp ^ code) & 1)
+        return ((shard + 16 + (step << 3)) & 24) | (step >> 2)
 
     copies = [
         pltpu.make_async_copy(row_hbm, row_ref, sems.at[0]),
@@ -217,46 +191,53 @@
 
     pl.semaphore_wait(barrier, FIRST + SECOND - 2)
 
-    def send(step, target):
-        pltpu.make_async_remote_copy(
-            src_ref=send1.at[step], dst_ref=recv1.at[step], send_sem=send1_sem, recv_sem=recv1_sem,
-            device_id=(grp, target), device_id_type=MESH,
-        ).start()
-
-    def produce(pair, targets):
+    def deliver(step, target):
+        @pl.when(target != shard)
+        def _():
+            pltpu.make_async_remote_copy(
+                src_ref=send1.at[step], dst_ref=recv1.at[shard], send_sem=send1_sem, recv_sem=recv1_sem,
+                device_id=(grp, target), device_id_type=MESH,
+            ).start()
+
+        @pl.when(target == shard)
+        def _():
+            recv1[shard] = send1[step]
+
+    def produce(pair, carry):
         first, second = 2 * pair, 2 * pair + 1
-        found = pick(targets[0]), pick(targets[1])
+        found = pick(peer1(first)), pick(peer1(second))
         send1[first], send1[second] = found
-        send(first, targets[0])
-
-        @pl.when(second < FIRST - 1)
+        deliver(first, peer1(first))
+        deliver(second, peer1(second))
+        return carry
+
+    lax.fori_loop(0, FIRST // 2, produce, 0)
+    sent = send1.at[pl.ds(0, FIRST - 1)]
+    pltpu.make_async_copy(sent, sent, recv1_sem).wait()
+    total = recv1[0]
+    for source in range(1, FIRST):
+        total = total + recv1[source]
+    for target in range(SECOND):
+        send2[target] = total[target : target + 1]
+    for target in range(SECOND):
+
+        @pl.when(target != grp)
         def _():
-            send(second, targets[1])
-
-        return peer1(first + 2), peer1(second + 2)
-
-    lax.fori_loop(0, FIRST // 2, produce, (peer1(0), peer1(1)))
-    pltpu.make_async_copy(recv1, recv1, recv1_sem).wait()
-    total = send1[FIRST - 1]
-    for step in range(FIRST - 1):
-        total = total + recv1[step]
-    for g in range(SECOND):
-        send2[g] = total[g : g + 1]
-    for step in range(SECOND - 1):
-        target = peer2(step)
-        pltpu.make_async_remote_copy(
-            src_ref=send2.at[target], dst_ref=recv2.at[step], send_sem=send2_sem, recv_sem=recv2_sem,
-            device_id=(target, shard), device_id_type=MESH,
-        ).start()
-    sent = send1.at[pl.ds(0, FIRST - 1)]
+            pltpu.make_async_remote_copy(
+                src_ref=send2.at[target], dst_ref=recv2.at[grp], send_sem=send2_sem, recv_sem=recv2_sem,
+                device_id=(target, shard), device_id_type=MESH,
+            ).start()
+
+    recv2[grp] = send2[grp]
     pltpu.make_async_copy(sent, sent, send1_sem).wait()
-    total = send2[grp]
-    pltpu.make_async_copy(recv2, recv2, recv2_sem).wait()
-    for step in range(SECOND - 1):
-        total = total + recv2[step]
+    others = send2.at[pl.ds(0, SECOND - 1)]
+    pltpu.make_async_copy(others, others, recv2_sem).wait()
+    total = recv2[0]
+    for source in range(1, SECOND):
+        total = total + recv2[source]
     for e in range(EXAMPLES):
         out_ref[e : e + 1, :] = total[:, NARROW * e : NARROW * e + KEPT // 256]
-    pltpu.make_async_copy(recv2, recv2, send2_sem).wait()
+    pltpu.make_async_copy(others, others, send2_sem).wait()
 
 
 def local(inputs, up_cotangent, signs, kept_row, kept_col):
@@ -280,9 +261,9 @@
             pltpu.VMEM((4, 2 * UNITS, 256), BF16),
             pltpu.VMEM((8 * COLS, 128), F32),
             pltpu.VMEM((FIRST, 8, 128), F32),
-            pltpu.VMEM((FIRST - 1, 8, 128), F32),
+            pltpu.VMEM((FIRST, 8, 128), F32),
             pltpu.VMEM((SECOND, 1, 128), F32),
-            pltpu.VMEM((SECOND - 1, 1, 128), F32),
+            pltpu.VMEM((SECOND, 1, 128), F32),
             pltpu.SemaphoreType.DMA((8,)),
             pltpu.SemaphoreType.DMA,
             pltpu.SemaphoreType.DMA,
@@ -290,9 +271,12 @@
             pltpu.SemaphoreType.DMA,
         ],
         compiler_params=pltpu.CompilerParams(
-            vmem_limit_bytes=64 << 20, collective_id=0, has_side_effects=True
+            vmem_limit_bytes=32 << 20, collective_id=0, has_side_effects=True
         ),
-    )(inputs, jnp.swapaxes(up_cotangent, 1, 2), signs, kept_row.reshape(64, 128), kept_col.reshape(64, 128))
+    )(*[
+        pltpu.with_memory_space_constraint(array, pltpu.HBM)
+        for array in (inputs, jnp.swapaxes(up_cotangent, 1, 2), signs, kept_row.reshape(64, 128), kept_col.reshape(64, 128))
+    ])
 
 
 def solution(mesh):

time: 26.9 us -> 23.3 us (0.87)
  Pallas kernels: 25.6 us -> 22.7 us
  local copies, waits for them, and re-layouts: 1.24 us -> 0.56 us
    pallas_call x1, Pallas kernels: 25.6 us -> 22.7 us  [local(): pl.pallas_call(kernel, out_shape=jax.ShapeDtypeStruct((EXAMPLES, KEPT //...]
    unnamed x1, local copies, waits for them, and re-layouts: 1.24 us -> 0.56 us
where the time goes in v5:
time: 23.3 us
  Pallas kernels  22.7 us (97%)
  local copies, waits for them, and re-layouts  0.56 us (2%)
    pallas_call x1, Pallas kernels, local(): pl.pallas_call(kernel, out_shape=jax.ShapeDtypeStruct((EXAMPLES, KEPT //...  22.7 us
    unnamed x1, local copies, waits for them, and re-layouts  0.56 us

profile of v5, /device:TPU:1, one launch (start us, length us, event | category | flops | bytes accessed | tf_op | source)
XLA Modules:
  0.0 23.3 jit_solution(2258473316237631463)
XLA Ops:
  0.0 22.7 %shard_map.55 = f32[2,32]{1,0:T(2,128)S(1)} custom-call(bf16[2,1024,512]{2,1,0:T(8,128)(2,1)} %x_hbm.1, bf16[2,448,1024]{2,1,0:T(8,128)(2,1)} %bitcast.3, s32[512,512]{1,0:T(8,128)} %s_hbm.1, s32[64,128]{1,0:T(8,128)} %bitcast.4, s32[64,128]{1,0:T(8,128)} %bitcast.5), custom_call_target="tpu_custom_call" | custom-call | tf_op jit(solution)/shard_map/pallas_call | solution.py:245
  22.7 0.6 %copy.7 = f32[2,32]{1,0:T(2,128)} copy(f32[2,32]{1,0:T(2,128)S(1)} %shard_map.55) | data formatting | bytes 512

commit v6 on v5

--- a/solution.py
+++ b/solution.py
@@ -69,7 +69,7 @@
 
 def kernel(
     x_hbm, c_hbm, s_hbm, row_hbm, col_hbm, out_ref,
-    x_ref, c_ref, s_ref, st_ref, row_ref, col_ref, q_vmem, q_smem, index_ref, sign_ref, split_ref, table,
+    x_ref, c_ref, s_ref, st_ref, row_ref, col_ref, q_vmem, q_smem, index_ref, sign_ref, split_ref, half_ref, table,
     send1, recv1, send2, recv2,
     sems, send1_sem, recv1_sem, send2_sem, recv2_sem,
 ):
@@ -77,7 +77,7 @@
     shard = lax.axis_index("shard")
 
     def peer1(step):
-        return ((shard + 16 + (step << 3)) & 24) | (step >> 2)
+        return ((shard + 8 + (step << 3)) & 24) | (step >> 2)
 
     copies = [
         pltpu.make_async_copy(row_hbm, row_ref, sems.at[0]),
@@ -101,7 +101,7 @@
     for step in range(1, SECOND):
         pl.semaphore_signal(barrier, inc=1, device_id=(grp ^ step, shard), device_id_type=MESH)
 
-    h256 = hadamard((256, 256))
+    h128 = hadamard((128, 128))
     lanes = lane_transform()
 
     copies[0].wait()
@@ -147,8 +147,6 @@
 
     copies[2].wait()
     st_ref[...] = jnp.transpose(s_ref[...].astype(F32))[:UNITS]
-    low_table = jnp.concatenate([h256, h256], axis=1)
-    high_table = jnp.concatenate([h256[:, : UNITS - 256], h256[:, : UNITS - 256]], axis=1)
     for e in range(EXAMPLES):
         copies[3 + 2 * e].wait()
         copies[4 + 2 * e].wait()
@@ -157,20 +155,28 @@
         a, b, c, d = t[0] + t[1], t[0] - t[1], t[2] + t[3], t[2] - t[3]
         part = slice(128 * e, 128 * e + 128)
         for j, value in enumerate((a + c, b + d, a - c, b - d)):
+            for block in range(4):
+                rows = slice(128 * block, min(128 * block + 128, UNITS))
+                high, low = split(value[rows])
+                size = high.shape[0]
+                split_ref[j, 256 * block : 256 * block + size, part] = high
+                split_ref[j, 256 * block + size : 256 * block + 2 * size, part] = low
+    full = jnp.concatenate([h128, h128], axis=1)
+    short = jnp.concatenate([h128[:, : UNITS - 384], h128[:, : UNITS - 384]], axis=1)
+    for j in range(4):
+        t = [dot(full, split_ref[j, 256 * block : 256 * block + 256]) for block in range(3)]
+        t.append(dot(short, split_ref[j, 768:]))
+        a, b, c, d = t[0] + t[1], t[0] - t[1], t[2] + t[3], t[2] - t[3]
+        for block, value in enumerate((a + c, b + d, a - c, b - d)):
+            rows = slice(128 * block, 128 * block + 128)
             high, low = split(value)
-            split_ref[j, :256, part] = high[:256]
-            split_ref[j, 256:512, part] = low[:256]
-            split_ref[j, 512 : 256 + UNITS, part] = high[256:]
-            split_ref[j, 256 + UNITS :, part] = low[256:]
+            half_ref[j, rows, :256] = high
+            half_ref[j, rows, 256:] = low
     lanes2 = jnp.concatenate([lanes, lanes], axis=0)
     for j in range(4):
-        first = dot(low_table, split_ref[j, :512])
-        second = dot(high_table, split_ref[j, 512:])
-        for upper, value in enumerate((first + second, first - second)):
-            high, low = split(value)
-            both = dot(jnp.concatenate([high, low], axis=1), lanes2)
-            table[pl.ds(2 * j * COLS + 256 * upper, 256)] = both[:, :128]
-            table[pl.ds((2 * j + 1) * COLS + 256 * upper, 256)] = both[:, 128:]
+        both = dot(half_ref[j], lanes2)
+        table[pl.ds(2 * j * COLS, COLS)] = both[:, :128]
+        table[pl.ds((2 * j + 1) * COLS, COLS)] = both[:, 128:]
     q_copy.wait()
 
     place = lane & (NARROW - 1)
@@ -217,9 +223,9 @@
     total = recv1[0]
     for source in range(1, FIRST):
         total = total + recv1[source]
-    for target in range(SECOND):
-        send2[target] = total[target : target + 1]
-    for target in range(SECOND):
+    for row in range(SECOND):
+        send2[row] = total[row : row + 1]
+    for target in (1, 0, 2, 3, 6, 7, 4, 5):
 
         @pl.when(target != grp)
         def _():
@@ -230,7 +236,7 @@
 
     recv2[grp] = send2[grp]
     pltpu.make_async_copy(sent, sent, send1_sem).wait()
-    others = send2.at[pl.ds(0, SECOND - 1)]
+    others = recv2.at[pl.ds(0, SECOND - 1)]
     pltpu.make_async_copy(others, others, recv2_sem).wait()
     total = recv2[0]
     for source in range(1, SECOND):
@@ -259,6 +265,7 @@
             pltpu.VMEM((64, PER_ROW, 8, 128), jnp.int32),
             pltpu.VMEM((FIRST, 8, 128), F32),
             pltpu.VMEM((4, 2 * UNITS, 256), BF16),
+            pltpu.VMEM((4, COLS, 512), BF16),
             pltpu.VMEM((8 * COLS, 128), F32),
             pltpu.VMEM((FIRST, 8, 128), F32),
             pltpu.VMEM((FIRST, 8, 128), F32),

time: 23.3 us -> 22.6 us (0.970)
  Pallas kernels: 22.7 us -> 22 us
    pallas_call x1, Pallas kernels: 22.7 us -> 22 us  [local(): pl.pallas_call(kernel, out_shape=jax.ShapeDtypeStruct((EXAMPLES, KEPT //...]
where the time goes in v6:
time: 22.6 us; the launch traced here: 22.5 us
  Pallas kernels  22 us (97%)
  local copies, waits for them, and re-layouts  0.56 us (2%)
    pallas_call x1, Pallas kernels, local(): pl.pallas_call(kernel, out_shape=jax.ShapeDtypeStruct((EXAMPLES, KEPT //...  22 us
    unnamed x1, local copies, waits for them, and re-layouts  0.56 us

profile of v6, /device:TPU:1, one launch (start us, length us, event | category | flops | bytes accessed | tf_op | source)
XLA Modules:
  0.0 22.5 jit_solution(3710760827825334325)
XLA Ops:
  0.0 22.0 %shard_map.55 = f32[2,32]{1,0:T(2,128)S(1)} custom-call(bf16[2,1024,512]{2,1,0:T(8,128)(2,1)} %x_hbm.1, bf16[2,448,1024]{2,1,0:T(8,128)(2,1)} %bitcast.3, s32[512,512]{1,0:T(8,128)} %s_hbm.1, s32[64,128]{1,0:T(8,128)} %bitcast.4, s32[64,128]{1,0:T(8,128)} %bitcast.5), custom_call_target="tpu_custom_call" | custom-call | tf_op jit(solution)/shard_map/pallas_call | solution.py:251
  22.0 0.6 %copy.7 = f32[2,32]{1,0:T(2,128)} copy(f32[2,32]{1,0:T(2,128)S(1)} %shard_map.55) | data formatting | bytes 512

commit v7 on v6

--- a/solution.py
+++ b/solution.py
@@ -94,10 +94,15 @@
     barrier = pltpu.get_barrier_semaphore()
 
     def greet(step, carry):
-        pl.semaphore_signal(barrier, inc=1, device_id=(grp, shard ^ step), device_id_type=MESH)
+        target = ((shard + (step << 3)) & 24) | (step >> 2)
+
+        @pl.when(target != shard)
+        def _():
+            pl.semaphore_signal(barrier, inc=1, device_id=(grp, target), device_id_type=MESH)
+
         return carry
 
-    lax.fori_loop(1, FIRST, greet, 0)
+    lax.fori_loop(0, FIRST, greet, 0)
     for step in range(1, SECOND):
         pl.semaphore_signal(barrier, inc=1, device_id=(grp ^ step, shard), device_id_type=MESH)
 
@@ -126,24 +131,19 @@
     q_vmem[...] = packed & 4095
     q_copy = pltpu.make_async_copy(q_vmem, q_smem, sems.at[7])
     q_copy.start()
-    sign = jnp.where((packed >> 18) == 1, -1.0, 1.0)
-    inner = ((packed >> 12) & (NARROW - 1)).astype(F32)
+    marks = (((packed >> 12) & (NARROW - 1)) | ((packed >> 18) << 7)).astype(F32)
     mine = (lane // PER_ROW) == sublane
 
     def diagonal(values):
         blocks = [jnp.where(mine, jnp.broadcast_to(values[r : r + 1], (8, 128)), 0.0) for r in range(64)]
         return jnp.concatenate(blocks, axis=0).astype(BF16)
 
-    spots = diagonal(inner)
-    for pair in range(PER_ROW // 2):
-        found = dot(spots, spread_table(256, lambda y: 2 * pair + (y >> 7))).astype(jnp.int32)
-        for u in range(2):
-            part = found[:, 128 * u : 128 * u + 128].reshape(64, 8, 128)
-            index_ref[:, 2 * pair + u] = part + (lane & NARROW)[None]
-    found = dot(diagonal(sign), spread_table(128, lambda y: y & (PER_ROW - 1))) * SCALE
+    found = dot(diagonal(marks), spread_table(128, lambda y: y & (PER_ROW - 1))).astype(jnp.int32)
     for r in range(FIRST):
         second_half = found[8 * (FIRST + r) : 8 * (FIRST + r) + 8]
-        sign_ref[r] = jnp.where((lane // PER_ROW) % 2 == 1, second_half, found[8 * r : 8 * r + 8])
+        mark = jnp.where((lane // PER_ROW) % 2 == 1, second_half, found[8 * r : 8 * r + 8])
+        index_ref[r] = (mark & (NARROW - 1)) | (lane & NARROW)
+        sign_ref[r] = jnp.where(mark >= 128, -SCALE, SCALE)
 
     copies[2].wait()
     st_ref[...] = jnp.transpose(s_ref[...].astype(F32))[:UNITS]
@@ -183,6 +183,7 @@
 
     def pick(target):
         block = ((target & 3) << 3) | (target >> 2)
+        index = index_ref[block]
         found = jnp.zeros((8, 128), F32)
         for half in range(2):
             r = block + half * FIRST
@@ -192,12 +193,12 @@
                     q = q_smem.at[:, pl.ds(i * PER_ROW + m, 1)][r, 0]
                     one = jnp.broadcast_to(table[pl.ds(q, 1), :], (8, 128))
                     rows = one if rows is None else jnp.where(sublane == i, one, rows)
-                found = jnp.where(place == half * PER_ROW + m, permute(rows, index_ref[r, m]), found)
+                found = jnp.where(place == half * PER_ROW + m, permute(rows, index), found)
         return found * sign_ref[block]
 
-    pl.semaphore_wait(barrier, FIRST + SECOND - 2)
-
-    def deliver(step, target):
+    def deliver(step, carry):
+        target = peer1(step)
+
         @pl.when(target != shard)
         def _():
             pltpu.make_async_remote_copy(
@@ -209,12 +210,24 @@
         def _():
             recv1[shard] = send1[step]
 
+        return carry
+
+    depth = shard & 7
+    meet = jnp.where(depth >= 4, 0, 9 - (5 * depth) // 2)
+
     def produce(pair, carry):
         first, second = 2 * pair, 2 * pair + 1
         found = pick(peer1(first)), pick(peer1(second))
         send1[first], send1[second] = found
-        deliver(first, peer1(first))
-        deliver(second, peer1(second))
+
+        @pl.when(pair == meet)
+        def _():
+            pl.semaphore_wait(barrier, FIRST + SECOND - 2)
+
+        @pl.when(pair >= meet)
+        def _():
+            lax.fori_loop(jnp.where(pair == meet, 0, first), second + 1, deliver, 0)
+
         return carry
 
     lax.fori_loop(0, FIRST // 2, produce, 0)
@@ -235,7 +248,6 @@
             ).start()
 
     recv2[grp] = send2[grp]
-    pltpu.make_async_copy(sent, sent, send1_sem).wait()
     others = recv2.at[pl.ds(0, SECOND - 1)]
     pltpu.make_async_copy(others, others, recv2_sem).wait()
     total = recv2[0]
@@ -243,6 +255,7 @@
         total = total + recv2[source]
     for e in range(EXAMPLES):
         out_ref[e : e + 1, :] = total[:, NARROW * e : NARROW * e + KEPT // 256]
+    pltpu.make_async_copy(sent, sent, send1_sem).wait()
     pltpu.make_async_copy(others, others, send2_sem).wait()
 
 
@@ -262,7 +275,7 @@
             pltpu.VMEM((64, 128), jnp.int32),
             pltpu.VMEM((64, 128), jnp.int32),
             pltpu.SMEM((64, 128), jnp.int32),
-            pltpu.VMEM((64, PER_ROW, 8, 128), jnp.int32),
+            pltpu.VMEM((FIRST, 8, 128), jnp.int32),
             pltpu.VMEM((FIRST, 8, 128), F32),
             pltpu.VMEM((4, 2 * UNITS, 256), BF16),
             pltpu.VMEM((4, COLS, 512), BF16),

time: 22.6 us -> 22.5 us (level)
  no operation moved by 1% of the time
where the time goes in v7:
time: 22.5 us; the launch traced here: 22.4 us
  Pallas kernels  21.8 us (97%)
  local copies, waits for them, and re-layouts  0.56 us (2%)
    pallas_call x1, Pallas kernels, local(): pl.pallas_call(kernel, out_shape=jax.ShapeDtypeStruct((EXAMPLES, KEPT //...  21.8 us
    unnamed x1, local copies, waits for them, and re-layouts  0.56 us

profile of v7, /device:TPU:1, one launch (start us, length us, event | category | flops | bytes accessed | tf_op | source)
XLA Modules:
  0.0 22.4 jit_solution(7779196423572886901)
XLA Ops:
  0.0 21.8 %shard_map.55 = f32[2,32]{1,0:T(2,128)S(1)} custom-call(bf16[2,1024,512]{2,1,0:T(8,128)(2,1)} %x_hbm.1, bf16[2,448,1024]{2,1,0:T(8,128)(2,1)} %bitcast.3, s32[512,512]{1,0:T(8,128)} %s_hbm.1, s32[64,128]{1,0:T(8,128)} %bitcast.4, s32[64,128]{1,0:T(8,128)} %bitcast.5), custom_call_target="tpu_custom_call" | custom-call | tf_op jit(solution)/shard_map/pallas_call | solution.py:264
  21.8 0.6 %copy.7 = f32[2,32]{1,0:T(2,128)} copy(f32[2,32]{1,0:T(2,128)S(1)} %shard_map.55) | data formatting | bytes 512

commit v8 on v7

--- a/solution.py
+++ b/solution.py
@@ -20,6 +20,7 @@
 SCALE = 1.0 / math.sqrt(4096 * 16384)
 FIRST = 32
 SECOND = 8
+DIRECT = 2
 NARROW = 64
 PER_ROW = 16
 
@@ -70,14 +71,16 @@
 def kernel(
     x_hbm, c_hbm, s_hbm, row_hbm, col_hbm, out_ref,
     x_ref, c_ref, s_ref, st_ref, row_ref, col_ref, q_vmem, q_smem, index_ref, sign_ref, split_ref, half_ref, table,
-    send1, recv1, send2, recv2,
-    sems, send1_sem, recv1_sem, send2_sem, recv2_sem,
+    send1, recv1, send2, recv2, send3, recv3,
+    sems, send1_sem, recv1_sem, send2_sem, recv2_sem, send3_sem, recv3_sem,
 ):
     grp = lax.axis_index("grp")
     shard = lax.axis_index("shard")
 
     def peer1(step):
-        return ((shard + 8 + (step << 3)) & 24) | (step >> 2)
+        group = step >> 2
+        depth = jnp.where(group < 4, group, 4 | ((shard & 3) ^ (7 - group)))
+        return ((shard + 8 + (step << 3)) & 24) | depth
 
     copies = [
         pltpu.make_async_copy(row_hbm, row_ref, sems.at[0]),
@@ -93,18 +96,29 @@
 
     barrier = pltpu.get_barrier_semaphore()
 
-    def greet(step, carry):
-        target = ((shard + (step << 3)) & 24) | (step >> 2)
-
-        @pl.when(target != shard)
-        def _():
-            pl.semaphore_signal(barrier, inc=1, device_id=(grp, target), device_id_type=MESH)
-
-        return carry
-
-    lax.fori_loop(0, FIRST, greet, 0)
-    for step in range(1, SECOND):
-        pl.semaphore_signal(barrier, inc=1, device_id=(grp ^ step, shard), device_id_type=MESH)
+    @pl.when(shard < DIRECT)
+    def _():
+        for depth in (4, 5, 6, 7, 3, 2, 1, 0):
+
+            def greet_all(n, carry):
+                peer = (grp ^ (n >> 2), shard ^ (((n & 3) << 3) | depth))
+                pl.semaphore_signal(barrier, inc=1, device_id=peer, device_id_type=MESH)
+                return carry
+
+            lax.fori_loop(0 if depth else 1, 4 * SECOND, greet_all, 0, unroll=4 if depth else 1)
+
+    @pl.when(shard >= DIRECT)
+    def _():
+        def greet(step, carry):
+            pl.semaphore_signal(barrier, inc=1, device_id=(grp, shard ^ step), device_id_type=MESH)
+            return carry
+
+        def greet_near(step, carry):
+            pl.semaphore_signal(barrier, inc=1, device_id=(grp ^ step, shard), device_id_type=MESH)
+            return carry
+
+        lax.fori_loop(1, FIRST, greet, 0)
+        lax.fori_loop(1, SECOND, greet_near, 0)
 
     h128 = hadamard((128, 128))
     lanes = lane_transform()
@@ -199,16 +213,40 @@
     def deliver(step, carry):
         target = peer1(step)
 
-        @pl.when(target != shard)
+        @pl.when((target >= DIRECT) & (target != shard))
         def _():
             pltpu.make_async_remote_copy(
                 src_ref=send1.at[step], dst_ref=recv1.at[shard], send_sem=send1_sem, recv_sem=recv1_sem,
                 device_id=(grp, target), device_id_type=MESH,
             ).start()
 
-        @pl.when(target == shard)
+        @pl.when((target >= DIRECT) & (target == shard))
         def _():
             recv1[shard] = send1[step]
+
+        @pl.when(target < DIRECT)
+        def _():
+            block = send1[step]
+            for g in range(SECOND):
+                send3[target, g] = block[g : g + 1]
+
+            def row(n, carry):
+                g = n ^ 1
+
+                @pl.when((target != shard) | (g != grp))
+                def _():
+                    pltpu.make_async_remote_copy(
+                        src_ref=send3.at[target, g], dst_ref=recv3.at[grp * FIRST + shard], send_sem=send3_sem,
+                        recv_sem=recv3_sem, device_id=(g, target), device_id_type=MESH,
+                    ).start()
+
+                @pl.when((target == shard) & (g == grp))
+                def _():
+                    recv3[grp * FIRST + shard] = send3[target, g]
+
+                return carry
+
+            lax.fori_loop(0, SECOND, row, 0)
 
         return carry
 
@@ -222,7 +260,7 @@
 
         @pl.when(pair == meet)
         def _():
-            pl.semaphore_wait(barrier, FIRST + SECOND - 2)
+            pl.semaphore_wait(barrier, FIRST + SECOND - 2 + (SECOND - 1) * jnp.where(shard < DIRECT, DIRECT - 1, DIRECT))
 
         @pl.when(pair >= meet)
         def _():
@@ -231,32 +269,50 @@
         return carry
 
     lax.fori_loop(0, FIRST // 2, produce, 0)
-    sent = send1.at[pl.ds(0, FIRST - 1)]
-    pltpu.make_async_copy(sent, sent, recv1_sem).wait()
-    total = recv1[0]
-    for source in range(1, FIRST):
-        total = total + recv1[source]
-    for row in range(SECOND):
-        send2[row] = total[row : row + 1]
-    for target in (1, 0, 2, 3, 6, 7, 4, 5):
-
-        @pl.when(target != grp)
-        def _():
-            pltpu.make_async_remote_copy(
-                src_ref=send2.at[target], dst_ref=recv2.at[grp], send_sem=send2_sem, recv_sem=recv2_sem,
-                device_id=(target, shard), device_id_type=MESH,
-            ).start()
-
-    recv2[grp] = send2[grp]
-    others = recv2.at[pl.ds(0, SECOND - 1)]
-    pltpu.make_async_copy(others, others, recv2_sem).wait()
-    total = recv2[0]
-    for source in range(1, SECOND):
-        total = total + recv2[source]
-    for e in range(EXAMPLES):
-        out_ref[e : e + 1, :] = total[:, NARROW * e : NARROW * e + KEPT // 256]
-    pltpu.make_async_copy(sent, sent, send1_sem).wait()
-    pltpu.make_async_copy(others, others, send2_sem).wait()
+    def awaited(buffer, count, semaphore):
+        part = buffer.at[pl.ds(0, count)]
+        pltpu.make_async_copy(part, part, semaphore).wait()
+
+    def finish(total):
+        for e in range(EXAMPLES):
+            out_ref[e : e + 1, :] = total[:, NARROW * e : NARROW * e + KEPT // 256]
+
+    @pl.when(shard < DIRECT)
+    def _():
+        awaited(recv3, FIRST * SECOND - 1, recv3_sem)
+        parts = [recv3[n] for n in range(4)]
+        for source in range(4, FIRST * SECOND):
+            parts[source % 4] = parts[source % 4] + recv3[source]
+        finish((parts[0] + parts[1]) + (parts[2] + parts[3]))
+        awaited(send1, FIRST - DIRECT, send1_sem)
+        awaited(recv3, DIRECT * SECOND - 1, send3_sem)
+
+    @pl.when(shard >= DIRECT)
+    def _():
+        awaited(recv1, FIRST - 1, recv1_sem)
+        total = recv1[0]
+        for source in range(1, FIRST):
+            total = total + recv1[source]
+        for target in range(SECOND):
+            send2[target] = total[target : target + 1]
+        for target in (1, 0, 2, 3, 6, 7, 4, 5):
+
+            @pl.when(target != grp)
+            def _():
+                pltpu.make_async_remote_copy(
+                    src_ref=send2.at[target], dst_ref=recv2.at[grp], send_sem=send2_sem, recv_sem=recv2_sem,
+                    device_id=(target, shard), device_id_type=MESH,
+                ).start()
+
+        recv2[grp] = send2[grp]
+        awaited(recv2, SECOND - 1, recv2_sem)
+        total = recv2[0]
+        for source in range(1, SECOND):
+            total = total + recv2[source]
+        finish(total)
+        awaited(send1, FIRST - DIRECT - 1, send1_sem)
+        awaited(recv3, DIRECT * SECOND, send3_sem)
+        awaited(recv2, SECOND - 1, send2_sem)
 
 
 def local(inputs, up_cotangent, signs, kept_row, kept_col):
@@ -284,7 +340,11 @@
             pltpu.VMEM((FIRST, 8, 128), F32),
             pltpu.VMEM((SECOND, 1, 128), F32),
             pltpu.VMEM((SECOND, 1, 128), F32),
+            pltpu.VMEM((DIRECT, SECOND, 1, 128), F32),
+            pltpu.VMEM((FIRST * SECOND, 1, 128), F32),
             pltpu.SemaphoreType.DMA((8,)),
+            pltpu.SemaphoreType.DMA,
+            pltpu.SemaphoreType.DMA,
             pltpu.SemaphoreType.DMA,
             pltpu.SemaphoreType.DMA,
             pltpu.SemaphoreType.DMA,

time: 22.5 us -> 21.8 us (0.969)
  the two profiles are of different devices: /device:TPU:1 before, /device:TPU:64 now
where the time goes in v8:
time: 21.8 us; the launch traced here: 21.7 us
  Pallas kernels  21.2 us (97%)
  local copies, waits for them, and re-layouts  0.56 us (3%)
    pallas_call x1, Pallas kernels, local(): pl.pallas_call(kernel, out_shape=jax.ShapeDtypeStruct((EXAMPLES, KEPT //...  21.2 us
    unnamed x1, local copies, waits for them, and re-layouts  0.56 us

profile of v8, /device:TPU:64, one launch (start us, length us, event | category | flops | bytes accessed | tf_op | source)
XLA Modules:
  0.0 21.7 jit_solution(4110784709479309839)
XLA Ops:
  0.0 21.2 %shard_map.55 = f32[2,32]{1,0:T(2,128)S(1)} custom-call(bf16[2,1024,512]{2,1,0:T(8,128)(2,1)} %x_hbm.1, bf16[2,448,1024]{2,1,0:T(8,128)(2,1)} %bitcast.3, s32[512,512]{1,0:T(8,128)} %s_hbm.1, s32[64,128]{1,0:T(8,128)} %bitcast.4, s32[64,128]{1,0:T(8,128)} %bitcast.5), custom_call_target="tpu_custom_call" | custom-call | tf_op jit(solution)/shard_map/pallas_call | solution.py:320
  21.2 0.6 %copy.7 = f32[2,32]{1,0:T(2,128)} copy(f32[2,32]{1,0:T(2,128)S(1)} %shard_map.55) | data formatting | bytes 512

commit v9 on v8

--- a/solution.py
+++ b/solution.py
@@ -230,28 +230,30 @@
             for g in range(SECOND):
                 send3[target, g] = block[g : g + 1]
 
-            def row(n, carry):
-                g = n ^ 1
-
-                @pl.when((target != shard) | (g != grp))
-                def _():
-                    pltpu.make_async_remote_copy(
-                        src_ref=send3.at[target, g], dst_ref=recv3.at[grp * FIRST + shard], send_sem=send3_sem,
-                        recv_sem=recv3_sem, device_id=(g, target), device_id_type=MESH,
-                    ).start()
-
-                @pl.when((target == shard) & (g == grp))
-                def _():
-                    recv3[grp * FIRST + shard] = send3[target, g]
-
-                return carry
-
-            lax.fori_loop(0, SECOND, row, 0)
+            def row(g):
+                return pltpu.make_async_remote_copy(
+                    src_ref=send3.at[target, g], dst_ref=recv3.at[grp * FIRST + shard], send_sem=send3_sem,
+                    recv_sem=recv3_sem, device_id=(g, target), device_id_type=MESH,
+                )
+
+            @pl.when(target != shard)
+            def _():
+                for g in (1, 0, 3, 2, 5, 4, 7, 6):
+                    row(g).start()
+
+            @pl.when(target == shard)
+            def _():
+                def inner(step, carry):
+                    row(grp ^ step).start()
+                    return carry
+
+                lax.fori_loop(1, SECOND, inner, 0)
+                recv3[grp * FIRST + shard] = send3[target, grp]
 
         return carry
 
     depth = shard & 7
-    meet = jnp.where(depth >= 4, 0, 9 - (5 * depth) // 2)
+    meet = jnp.where(depth >= 4, 0, 12 - 3 * depth)
 
     def produce(pair, carry):
         first, second = 2 * pair, 2 * pair + 1

time: 21.8 us -> 21.8 us (level)
  no operation moved by 1% of the time
where the time goes in v9:
time: 21.8 us; the launch traced here: 21.7 us
  Pallas kernels  21.1 us (97%)
  local copies, waits for them, and re-layouts  0.56 us (3%)
    pallas_call x1, Pallas kernels, local(): pl.pallas_call(kernel, out_shape=jax.ShapeDtypeStruct((EXAMPLES, KEPT //...  21.1 us
    unnamed x1, local copies, waits for them, and re-layouts  0.56 us

profile of v9, /device:TPU:64, one launch (start us, length us, event | category | flops | bytes accessed | tf_op | source)
XLA Modules:
  0.0 21.7 jit_solution(3323184595293908415)
XLA Ops:
  0.0 21.1 %shard_map.55 = f32[2,32]{1,0:T(2,128)S(1)} custom-call(bf16[2,1024,512]{2,1,0:T(8,128)(2,1)} %x_hbm.1, bf16[2,448,1024]{2,1,0:T(8,128)(2,1)} %bitcast.3, s32[512,512]{1,0:T(8,128)} %s_hbm.1, s32[64,128]{1,0:T(8,128)} %bitcast.4, s32[64,128]{1,0:T(8,128)} %bitcast.5), custom_call_target="tpu_custom_call" | custom-call | tf_op jit(solution)/shard_map/pallas_call | solution.py:322
  21.2 0.6 %copy.7 = f32[2,32]{1,0:T(2,128)} copy(f32[2,32]{1,0:T(2,128)S(1)} %shard_map.55) | data formatting | bytes 512
